TPU v7x, 256 devices: a whole 4x4x8 slice. The times are simulated.
256 devices in a mesh: gx: 16 (over y, x), gy: 16 (over z, core).
Axes of the slice: x: 4, y: 4, z: 8, core: 2. Of those that a mesh axis runs over, the one named last changes fastest.
Arguments:
- vectors: float32 [8, 128, 256, 256], P(None, 'gx', 'gy'), may hold values from -10 to 10
- weight_x: float32 [128, 256, 256], P('gx', 'gy'), may hold values from 0.05 to 1
- weight_y: float32 [128, 256, 256], P('gx', 'gy'), may hold values from 0.05 to 1
- weight_z: float32 [128, 256, 256], P('gx', 'gy'), may hold values from 0.05 to 1
Outputs:
- refined: float32 [8, 128, 256, 256], P(None, 'gx', 'gy')
- eigenvalues: float32 [8], replicated
All inputs are finite; a program needn't handle non-finite values.
Results may differ from a plain program's by a relative error of at most 0.000075.
Values sent between devices are 32-bit elements; how exact they have to be, the bound alone decides.
No kernel may reach another device: no remote copies, remote signals or barrier semaphores. Data moves between devices by JAX's collectives and lax.ppermute only.
A program may use at most 128 MiB of HBM per device.

v0:
```python
import jax
import jax.numpy as jnp
from jax import lax
from jax.sharding import PartitionSpec as P

COARSE_SWEEPS = 4
OMEGA = 0.8
SHIFT = 0.1


def shifted(shard, axis, by):
    count = lax.axis_size(axis)
    pairs = [(i, i + by) for i in range(count) if 0 <= i + by < count]
    return lax.ppermute(shard, axis, pairs)


def with_halo(cells, sides, width):
    for axis, dim in sides:
        count = lax.axis_size(axis)
        ends = count - 1
        head = lax.slice_in_dim(cells, 0, width, axis=dim)
        tail = lax.slice_in_dim(cells, cells.shape[dim] - width, cells.shape[dim], axis=dim)
        cells = jnp.concatenate(
            [
                lax.ppermute(tail, axis, [(i, (i + 1) % count) for i in range(ends)]),
                cells,
                lax.ppermute(head, axis, [((i + 1) % count, i) for i in range(ends)]),
            ],
            axis=dim,
        )
    return cells


def lower_x(weights):
    rim = shifted(weights[-1:], "gx", 1)
    return jnp.concatenate([rim, weights[:-1]], 0)


def lower_y(weights):
    rim = shifted(weights[:, -1:], "gy", 1)
    return jnp.concatenate([rim, weights[:, :-1]], 1)


def lower_z(weights):
    return jnp.concatenate([jnp.zeros_like(weights[:, :, :1]), weights[:, :, :-1]], 2)


def trimmed(array):
    return array[..., 1:-1, 1:-1, :]


def inner_sum(field, parts):
    wx, lx, wy, ly, wz, lz = parts
    centre = trimmed(field)
    zpadded = jnp.pad(centre, ((0, 0), (0, 0), (0, 0), (1, 1)))
    total = wx[None] * field[:, 2:, 1:-1] + lx[None] * field[:, :-2, 1:-1]
    total = total + wy[None] * field[:, 1:-1, 2:] + ly[None] * field[:, 1:-1, :-2]
    total = total + wz[None] * zpadded[..., 2:] + lz[None] * zpadded[..., :-2]
    return total


def neighbours(field, parts, level):
    if level == "fine":
        padded = with_halo(field, (("gx", 1), ("gy", 2)), 1)
    else:
        padded = with_halo(field, (("gx", 1), ("gy", 2)), 1)
    return inner_sum(padded, parts)


def jacobi(guess, source, diag, parts, level):
    return (
        guess
        + OMEGA * (source - (diag[None] * guess - neighbours(guess, parts, level))) / diag[None]
    )


def rayleigh_sums(vectors, applied, degree):
    return lax.psum(
        (
            jnp.sum(vectors * applied, axis=(1, 2, 3)),
            jnp.sum(vectors * (degree[None] * vectors), axis=(1, 2, 3)),
        ),
        ("gx", "gy"),
    )


def coarse_weights(wx, wy, wz, degree):
    sx, sy, sz = wx.shape
    shape = (sx // 2, 2, sy // 2, 2, sz // 2, 2)
    cx = wx.reshape(shape)[:, 1].sum(axis=(2, 4))
    cy = wy.reshape(shape)[:, :, :, 1].sum(axis=(1, 4))
    cz = wz.reshape(shape)[..., 1].sum(axis=(1, 3))
    dsum = degree.reshape(shape).sum(axis=(1, 3, 5))
    return (cx, cy, cz, dsum)


def restrict(field):
    kk, sx, sy, sz = field.shape
    return field.reshape(kk, sx // 2, 2, sy // 2, 2, sz // 2, 2).sum(axis=(2, 4, 6))


def prolong(field):
    kk, sx, sy, sz = field.shape
    return jnp.broadcast_to(field[:, :, None, :, None, :, None], (kk, sx, 2, sy, 2, sz, 2)).reshape(
        kk, 2 * sx, 2 * sy, 2 * sz
    )


def per_device(vectors, weight_x, weight_y, weight_z):
    local_x, local_y, depth = weight_x.shape
    span_x = local_x * lax.axis_size("gx")
    span_y = local_y * lax.axis_size("gy")
    pos_x = lax.axis_index("gx") * local_x + lax.broadcasted_iota(jnp.int32, (local_x, 1, 1), 0)
    pos_y = lax.axis_index("gy") * local_y + lax.broadcasted_iota(jnp.int32, (1, local_y, 1), 1)
    pos_z = lax.broadcasted_iota(jnp.int32, (1, 1, depth), 2)
    wx = jnp.where(pos_x < span_x - 1, weight_x, jnp.zeros_like(weight_x))
    wy = jnp.where(pos_y < span_y - 1, weight_y, jnp.zeros_like(weight_y))
    wz = jnp.where(pos_z < depth - 1, weight_z, jnp.zeros_like(weight_z))
    parts = (wx, lower_x(wx), wy, lower_y(wy), wz, lower_z(wz))
    degree = parts[0] + parts[1] + parts[2] + parts[3] + parts[4] + parts[5]
    applied = degree[None] * vectors - neighbours(vectors, parts, "fine")
    numer, denom = rayleigh_sums(vectors, applied, degree)
    eigenvalues = numer / denom
    resid = applied - eigenvalues[:, None, None, None] * (degree[None] * vectors)
    dfine = (1.0 + SHIFT) * degree
    guess = OMEGA * resid / dfine[None]
    guess = jacobi(guess, resid, dfine, parts, "fine")
    fine_rest = resid - (dfine[None] * guess - neighbours(guess, parts, "fine"))
    cx, cy, cz, dsum = coarse_weights(wx, wy, wz, degree)
    cparts = (cx, lower_x(cx), cy, lower_y(cy), cz, lower_z(cz))
    dcoarse = cparts[0] + cparts[1] + cparts[2] + cparts[3] + cparts[4] + cparts[5] + SHIFT * dsum
    rcoarse = restrict(fine_rest)
    correction = OMEGA * rcoarse / dcoarse[None]
    for sweep in range(COARSE_SWEEPS - 1):
        correction = jacobi(correction, rcoarse, dcoarse, cparts, "coarse")
    guess = guess + prolong(correction)
    guess = jacobi(guess, resid, dfine, parts, "fine")
    updated = vectors - guess
    local_gram = jnp.einsum(
        "aijk,bijk->ab", updated, degree[None] * updated, precision=lax.Precision.HIGHEST
    )
    gram = lax.psum(local_gram, ("gx", "gy"))
    gram = gram / (span_x * span_y * depth)
    chol = jnp.linalg.cholesky(gram)
    flat = updated.reshape(updated.shape[0], -1)
    refined = jax.scipy.linalg.solve_triangular(chol, flat, lower=True).reshape(updated.shape)
    return (refined, eigenvalues)


def solution(mesh):
    return jax.shard_map(
        per_device,
        mesh=mesh,
        in_specs=(
            P(None, "gx", "gy", None),
            P("gx", "gy", None),
            P("gx", "gy", None),
            P("gx", "gy", None),
        ),
        out_specs=(P(None, "gx", "gy", None), P()),
        check_vma=False,
    )
```

profile of v0, /device:TPU:1, one launch (start us, length us, event | category | flops | bytes accessed | tf_op | source)
XLA Modules:
  0.0 427.5 jit_solution(8508537190117706973)
XLA Ops:
  1.7 3.9 collective-permute-start
  6.6 4.4 %collective-permute-start.1 = (f32[8,1,256]{2,1,0:T(1,128)S(1)}, f32[8,1,256]{2,1,0:T(1,128)S(1)}, u32[]{:S(2)}, u32[]{:S(2)}) collective-permute-start(f32[8,1,256]{2,1,0:T(1,128)S(1)} %slice.374), channel_id=1, source_target_pairs={{0,1},{1,2},{2,3},{3,4},{4,5},{5,6},{6,7},{7,8},{8,9},{9,10},{10,1... | collective-permute-start | bytes 24584 | tf_op jit(solution)/shard_map/ppermute | solution.py:14
  12.0 3.1 collective-permute-start.3
  16.5 9.8 %reshape.74 = f32[4,2,8,2,128,2]{5,4,3,2,1,0:T(8,128)} reshape(f32[8,16,256]{2,1,0:T(8,128)S(1)} %broadcast_select_fusion.2) | data formatting | bytes 262144 | tf_op jit(solution)/shard_map/reshape | solution.py:90
  26.6 1.9 collective-permute-start.4
  28.6 3.6 collective-permute-start.5
  33.8 2.1 fusion
  35.9 82.2 %all-reduce.9 = (f32[8]{0:T(128)S(1)}, f32[8]{0:T(128)S(1)}) all-reduce(f32[8]{0:T(128)S(1)} %get-tuple-element.19, f32[8]{0:T(128)S(1)} %get-tuple-element.18), channel_id=1, replica_groups=mesh['gx'=16,'gy'=16] {'gx','gy'}, use_global_device_ids=true, to_apply=%region_1.2 | all-reduce | flops 16 | bytes 128 | tf_op jit(solution)/shard_map/psum | solution.py:78
  118.1 1.7 multiply_divide_fusion
  121.8 4.7 %collective-permute-start.7 = (f32[8,1,16,256]{3,2,1,0:T(8,128)}, f32[8,1,16,256]{3,2,1,0:T(8,128)}, u32[]{:S(2)}, u32[]{:S(2)}) collective-permute-start(f32[8,1,16,256]{3,2,1,0:T(8,128)} %get-tuple-element.44), channel_id=1, source_target_pairs={{0,16},{16,32},{32,48},{48,64},{64,80},{80,96},{96,112},{112,128},... | collective-permute-start | bytes 393224 | tf_op jit(solution)/shard_map/ppermute | solution.py:25
  126.5 2.8 slice_reduce_fusion.2
  130.5 2.5 collective-permute-start.14
  133.0 9.7 %reshape.75 = f32[4,2,8,2,128,2]{5,4,3,2,1,0:T(8,128)} reshape(f32[8,16,256]{2,1,0:T(8,128)S(1)} %broadcast_select_fusion.1) | data formatting | bytes 262144 | tf_op jit(solution)/shard_map/reshape | solution.py:91
  143.8 3.4 collective-permute-start.8
  147.2 2.9 collective-permute-start.9
  150.1 2.8 slice_reduce_fusion.1
  153.5 2.5 collective-permute-start.15
  156.1 9.8 %reshape.76 = f32[4,2,8,2,128,2]{5,4,3,2,1,0:T(8,128)} reshape(f32[8,16,256]{2,1,0:T(8,128)S(1)} %broadcast_select_fusion) | data formatting | bytes 262144 | tf_op jit(solution)/shard_map/reshape | solution.py:92
  166.1 5.3 %fusion.13 = f32[8,8,16,256]{3,2,1,0:T(8,128)S(1)} fusion(f32[8,8,16,256]{3,2,1,0:T(8,128)} %copy-done.1, f32[8,8,16,256]{3,2,1,0:T(8,128)S(1)} %get-tuple-element.27, f32[8,10,1,256]{3,2,1,0:T(1,128)S(1)} %copy.441, f32[8,1,16,256]{3,2,1,0:T(8,128)} %copy-done.25, f32[8,1,16,256]{3,2,1,0:T(8,128)} %collective-permute-done.7, ...), kind=kLoop, calls=%fused_computation.28 | loop fusion | flops 6553600 | bytes 4489216 | tf_op jit(solution)/shard_map/add | solution.py:72
  173.4 4.7 %collective-permute-start.11 = (f32[8,1,16,256]{3,2,1,0:T(8,128)}, f32[8,1,16,256]{3,2,1,0:T(8,128)}, u32[]{:S(2)}, u32[]{:S(2)}) collective-permute-start(f32[8,1,16,256]{3,2,1,0:T(8,128)} %get-tuple-element.42), channel_id=1, source_target_pairs={{0,16},{16,32},{32,48},{48,64},{64,80},{80,96},{96,112},{112,128},... | collective-permute-start | bytes 393224 | tf_op jit(solution)/shard_map/ppermute | solution.py:25
  178.1 6.8 %slice_reduce_fusion = f32[4,8,128]{2,1,0:T(8,128)} fusion(f32[4,2,8,2,128,2]{5,4,3,2,1,0:T(8,128)} %reshape.76), kind=kLoop, calls=%fused_computation | loop fusion | flops 12288 | bytes 81920 | tf_op jit(solution)/shard_map/reduce_sum | solution.py:92
  184.8 10.5 %reshape.77 = f32[4,2,8,2,128,2]{5,4,3,2,1,0:T(8,128)} reshape(f32[8,16,256]{2,1,0:T(8,128)} %copy-done.8) | data formatting | bytes 262144 | tf_op jit(solution)/shard_map/reshape | solution.py:93
  195.3 4.6 %reduce_sum.69 = f32[4,8,128]{2,1,0:T(8,128)} reduce(f32[4,2,8,2,128,2]{5,4,3,2,1,0:T(8,128)} %reshape.77, f32[]{:T(128)} %constant.65.clone.1), dimensions={1,3,5}, to_apply=%region_8.9 | reduce | flops 28672 | bytes 147460 | tf_op jit(solution)/shard_map/reduce_sum | solution.py:93
  201.2 3.0 collective-permute-start.12
  204.3 2.5 collective-permute-start.13
  208.5 2.8 fusion.19
  211.3 9.8 %copy.446 = f32[8,8,16,256]{0,3,2,1:T(8,128)} copy(f32[8,8,16,256]{3,2,1,0:T(8,128)} %fusion.19) | data formatting | bytes 2097152 | tf_op jit(solution)/shard_map/sub | solution.py:128
  221.1 13.1 %reduce_sum.65 = f32[8,4,8,128]{0,3,2,1:T(8,128)} reduce(f32[8,4,2,8,2,128,2]{0,6,5,4,3,2,1:T(2,128)} %bitcast.30, f32[]{:T(128)} %constant.65.clone.1), dimensions={2,4,6}, to_apply=%region_4.5 | reduce | flops 229376 | bytes 1179652 | tf_op jit(solution)/shard_map/reduce_sum | solution.py:99
  234.2 2.8 copy.447
  239.4 4.0 collective-permute-start.17
  244.4 2.9 collective-permute-start.18
  247.4 4.3 %collective-permute-start.19 = (f32[8,6,1,128]{3,2,1,0:T(1,128)S(1)}, f32[8,6,1,128]{3,2,1,0:T(1,128)S(1)}, u32[]{:S(2)}, u32[]{:S(2)}) collective-permute-start(f32[8,6,1,128]{3,2,1,0:T(1,128)S(1)} %get-tuple-element.53), channel_id=1, source_target_pairs={{0,1},{1,2},{2,3},{3,4},{4,5},{5,6},{6,7},{7,8},{8,9},{9,10},{10,1... | collective-permute-start | bytes 73736 | tf_op jit(solution)/shard_map/ppermute | solution.py:25
  255.1 4.6 %collective-permute-start.21 = (f32[8,1,8,128]{3,2,1,0:T(8,128)S(1)}, f32[8,1,8,128]{3,2,1,0:T(8,128)S(1)}, u32[]{:S(2)}, u32[]{:S(2)}) collective-permute-start(f32[8,1,8,128]{3,2,1,0:T(8,128)S(1)} %get-tuple-element.56), channel_id=1, source_target_pairs={{0,16},{16,32},{32,48},{48,64},{64,80},{80,96},{96,112},{112,128},... | collective-permute-start | bytes 98312 | tf_op jit(solution)/shard_map/ppermute | solution.py:25
  260.7 1.9 collective-permute-start.22
  262.6 5.1 %collective-permute-start.23 = (f32[8,6,1,128]{3,2,1,0:T(1,128)S(1)}, f32[8,6,1,128]{3,2,1,0:T(1,128)S(1)}, u32[]{:S(2)}, u32[]{:S(2)}) collective-permute-start(f32[8,6,1,128]{3,2,1,0:T(1,128)S(1)} %get-tuple-element.51), channel_id=1, source_target_pairs={{0,1},{1,2},{2,3},{3,4},{4,5},{5,6},{6,7},{7,8},{8,9},{9,10},{10,1... | collective-permute-start | bytes 73736 | tf_op jit(solution)/shard_map/ppermute | solution.py:25
  270.1 4.6 %collective-permute-start.25 = (f32[8,1,8,128]{3,2,1,0:T(8,128)S(1)}, f32[8,1,8,128]{3,2,1,0:T(8,128)S(1)}, u32[]{:S(2)}, u32[]{:S(2)}) collective-permute-start(f32[8,1,8,128]{3,2,1,0:T(8,128)S(1)} %get-tuple-element.54), channel_id=1, source_target_pairs={{0,16},{16,32},{32,48},{48,64},{64,80},{80,96},{96,112},{112,128},... | collective-permute-start | bytes 98312 | tf_op jit(solution)/shard_map/ppermute | solution.py:25
  275.8 1.9 collective-permute-start.26
  277.7 5.1 %collective-permute-start.27 = (f32[8,6,1,128]{3,2,1,0:T(1,128)S(1)}, f32[8,6,1,128]{3,2,1,0:T(1,128)S(1)}, u32[]{:S(2)}, u32[]{:S(2)}) collective-permute-start(f32[8,6,1,128]{3,2,1,0:T(1,128)S(1)} %get-tuple-element.49), channel_id=1, source_target_pairs={{0,1},{1,2},{2,3},{3,4},{4,5},{5,6},{6,7},{7,8},{8,9},{9,10},{10,1... | collective-permute-start | bytes 73736 | tf_op jit(solution)/shard_map/ppermute | solution.py:25
  284.5 2.9 copy.451
  287.4 7.1 %broadcast_in_dim.30 = f32[8,4,2,8,2,128,2]{0,6,5,4,3,2,1:T(2,128)} broadcast(f32[8,4,8,128]{0,3,2,1:T(8,128)} %copy.451), dimensions={0,1,3,5} | broadcast | bytes 1179648 | tf_op jit(solution)/shard_map/broadcast_in_dim | solution.py:104
  294.5 10.6 %copy.452 = f32[8,8,16,256]{3,2,1,0:T(8,128)} copy(f32[8,8,16,256]{0,3,2,1:T(8,128)} %bitcast.31) | data formatting | bytes 2097152 | tf_op jit(solution)/shard_map/reshape | solution.py:104
  308.1 4.6 %collective-permute-start.29 = (f32[8,1,16,256]{3,2,1,0:T(8,128)S(1)}, f32[8,1,16,256]{3,2,1,0:T(8,128)S(1)}, u32[]{:S(2)}, u32[]{:S(2)}) collective-permute-start(f32[8,1,16,256]{3,2,1,0:T(8,128)S(1)} %get-tuple-element.40), channel_id=1, source_target_pairs={{0,16},{16,32},{32,48},{48,64},{64,80},{80,96},{96,112},{112,128},... | collective-permute-start | bytes 393224 | tf_op jit(solution)/shard_map/ppermute | solution.py:25
  313.1 1.5 collective-permute-done.29
  314.7 1.9 collective-permute-start.30
  316.7 5.3 %collective-permute-start.31 = (f32[8,10,1,256]{3,0,2,1:T(8,128)S(1)}, f32[8,10,1,256]{3,0,2,1:T(8,128)S(1)}, u32[]{:S(2)}, u32[]{:S(2)}) collective-permute-start(f32[8,10,1,256]{3,0,2,1:T(8,128)S(1)} %copy.455), channel_id=1, source_target_pairs={{0,1},{1,2},{2,3},{3,4},{4,5},{5,6},{6,7},{7,8},{8,9},{9,10},{10,1... | collective-permute-start | bytes 245768 | tf_op jit(solution)/shard_map/ppermute | solution.py:25
  323.3 1.6 broadcast_multiply_fusion
  324.9 3.0 convolution_bitcast_fusion
  327.9 93.9 %psum.23 = f32[8,8]{0,1:T(8,128)S(1)} all-reduce(f32[8,8]{0,1:T(8,128)S(1)} %convolution_bitcast_fusion), channel_id=1, replica_groups=mesh['gx'=16,'gy'=16] {'gx','gy'}, use_global_device_ids=true, to_apply=%region_9.10 | all-reduce | flops 64 | bytes 512 | tf_op jit(solution)/shard_map/psum | solution.py:142
  (174 shorter events, 39.2 us)
Async XLA Ops:
  1.6 24.6 %copy-start.2 = (f32[8,16,256]{2,1,0:T(8,128)}, f32[8,16,256]{2,1,0:T(8,128)S(1)}, u32[]{:S(2)}) copy-start(f32[8,16,256]{2,1,0:T(8,128)S(1)} %broadcast_select_fusion.2) | copy-start | bytes 393220
  1.7 30.6 %collective-permute-start = (f32[1,16,256]{2,1,0:T(8,128)S(1)}, f32[1,16,256]{2,1,0:T(8,128)S(1)}, u32[]{:S(2)}, u32[]{:S(2)}) collective-permute-start(f32[1,16,256]{2,1,0:T(8,128)S(1)} %slice.372), channel_id=1, source_target_pairs={{0,16},{16,32},{32,48},{48,64},{64,80},{80,96},{96,112},{112,128},... | collective-permute-start | bytes 49160 | tf_op jit(solution)/shard_map/ppermute | solution.py:14
  6.6 25.6 %collective-permute-start.1 = (f32[8,1,256]{2,1,0:T(1,128)S(1)}, f32[8,1,256]{2,1,0:T(1,128)S(1)}, u32[]{:S(2)}, u32[]{:S(2)}) collective-permute-start(f32[8,1,256]{2,1,0:T(1,128)S(1)} %slice.374), channel_id=1, source_target_pairs={{0,1},{1,2},{2,3},{3,4},{4,5},{5,6},{6,7},{7,8},{8,9},{9,10},{10,1... | collective-permute-start | bytes 24584 | tf_op jit(solution)/shard_map/ppermute | solution.py:14
  12.0 14.3 %collective-permute-start.3 = (f32[8,1,16,256]{3,2,1,0:T(8,128)S(1)}, f32[8,1,16,256]{3,2,1,0:T(8,128)S(1)}, u32[]{:S(2)}, u32[]{:S(2)}) collective-permute-start(f32[8,1,16,256]{3,2,1,0:T(8,128)S(1)} %get-tuple-element.47), channel_id=1, source_target_pairs={{0,16},{16,32},{32,48},{48,64},{64,80},{80,96},{96,112},{112,128},... | collective-permute-start | bytes 393224 | tf_op jit(solution)/shard_map/ppermute | solution.py:25
  15.2 11.3 %collective-permute-start.2 = (f32[8,1,16,256]{3,2,1,0:T(8,128)S(1)}, f32[8,1,16,256]{3,2,1,0:T(8,128)S(1)}, u32[]{:S(2)}, u32[]{:S(2)}) collective-permute-start(f32[8,1,16,256]{3,2,1,0:T(8,128)S(1)} %get-tuple-element.46), channel_id=1, source_target_pairs={{16,0},{32,16},{48,32},{64,48},{80,64},{96,80},{112,96},{128,112},... | collective-permute-start | bytes 393224 | tf_op jit(solution)/shard_map/ppermute | solution.py:27
  26.6 6.4 %collective-permute-start.4 = (f32[8,10,1,256]{3,0,2,1:T(8,128)S(1)}, f32[8,10,1,256]{3,0,2,1:T(8,128)S(1)}, u32[]{:S(2)}, u32[]{:S(2)}) collective-permute-start(f32[8,10,1,256]{3,0,2,1:T(8,128)S(1)} %copy.466), channel_id=1, source_target_pairs={{1,0},{2,1},{3,2},{4,3},{5,4},{6,5},{7,6},{8,7},{9,8},{10,9},{11,1... | collective-permute-start | bytes 245768 | tf_op jit(solution)/shard_map/ppermute | solution.py:27
  28.6 5.1 %collective-permute-start.5 = (f32[8,10,1,256]{3,0,2,1:T(8,128)S(1)}, f32[8,10,1,256]{3,0,2,1:T(8,128)S(1)}, u32[]{:S(2)}, u32[]{:S(2)}) collective-permute-start(f32[8,10,1,256]{3,0,2,1:T(8,128)S(1)} %copy.467), channel_id=1, source_target_pairs={{0,1},{1,2},{2,3},{3,4},{4,5},{5,6},{6,7},{7,8},{8,9},{9,10},{10,1... | collective-permute-start | bytes 245768 | tf_op jit(solution)/shard_map/ppermute | solution.py:25
  33.8 84.3 %copy-start.5 = (f32[8,16,256]{2,1,0:T(8,128)S(1)}, f32[8,16,256]{2,1,0:T(8,128)}, u32[]{:S(2)}) copy-start(f32[8,16,256]{2,1,0:T(8,128)} %get-tuple-element.28) | copy-start | bytes 393220
  119.8 22.9 %copy-start.1 = (f32[8,8,16,256]{3,2,1,0:T(8,128)}, f32[8,8,16,256]{3,2,1,0:T(8,128)S(1)}, u32[]{:S(2)}) copy-start(f32[8,8,16,256]{3,2,1,0:T(8,128)S(1)} %get-tuple-element.26) | copy-start | bytes 3145732
  120.6 22.2 %collective-permute-start.6 = (f32[8,1,16,256]{3,2,1,0:T(8,128)}, f32[8,1,16,256]{3,2,1,0:T(8,128)S(1)}, u32[]{:S(2)}, u32[]{:S(2)}) collective-permute-start(f32[8,1,16,256]{3,2,1,0:T(8,128)} %get-tuple-element.45), channel_id=1, source_target_pairs={{16,0},{32,16},{48,32},{64,48},{80,64},{96,80},{112,96},{128,112},... | collective-permute-start | bytes 393224 | tf_op jit(solution)/shard_map/ppermute | solution.py:27
  121.8 20.9 %collective-permute-start.7 = (f32[8,1,16,256]{3,2,1,0:T(8,128)}, f32[8,1,16,256]{3,2,1,0:T(8,128)}, u32[]{:S(2)}, u32[]{:S(2)}) collective-permute-start(f32[8,1,16,256]{3,2,1,0:T(8,128)} %get-tuple-element.44), channel_id=1, source_target_pairs={{0,16},{16,32},{32,48},{48,64},{64,80},{80,96},{96,112},{112,128},... | collective-permute-start | bytes 393224 | tf_op jit(solution)/shard_map/ppermute | solution.py:25
  130.5 76.3 %collective-permute-start.14 = (f32[1,8,128]{2,1,0:T(8,128)}, f32[1,8,128]{2,1,0:T(8,128)}, u32[]{:S(2)}, u32[]{:S(2)}) collective-permute-start(f32[1,8,128]{2,1,0:T(8,128)} %slice.384), channel_id=1, source_target_pairs={{0,16},{16,32},{32,48},{48,64},{64,80},{80,96},{96,112},{112,128},... | collective-permute-start | bytes 12296 | tf_op jit(solution)/shard_map/ppermute | solution.py:14
  143.8 22.1 %collective-permute-start.8 = (f32[8,10,1,256]{3,0,2,1:T(8,128)S(1)}, f32[8,10,1,256]{3,0,2,1:T(8,128)S(1)}, u32[]{:S(2)}, u32[]{:S(2)}) collective-permute-start(f32[8,10,1,256]{3,0,2,1:T(8,128)S(1)} %copy.438), channel_id=1, source_target_pairs={{1,0},{2,1},{3,2},{4,3},{5,4},{6,5},{7,6},{8,7},{9,8},{10,9},{11,1... | collective-permute-start | bytes 245768 | tf_op jit(solution)/shard_map/ppermute | solution.py:27
  147.2 18.7 %collective-permute-start.9 = (f32[8,10,1,256]{3,0,2,1:T(8,128)S(1)}, f32[8,10,1,256]{3,0,2,1:T(8,128)S(1)}, u32[]{:S(2)}, u32[]{:S(2)}) collective-permute-start(f32[8,10,1,256]{3,0,2,1:T(8,128)S(1)} %copy.440), channel_id=1, source_target_pairs={{0,1},{1,2},{2,3},{3,4},{4,5},{5,6},{6,7},{7,8},{8,9},{9,10},{10,1... | collective-permute-start | bytes 245768 | tf_op jit(solution)/shard_map/ppermute | solution.py:25
  153.5 12.5 %copy-start.4 = (f32[8,16,256]{2,1,0:T(8,128)S(1)}, f32[8,16,256]{2,1,0:T(8,128)}, u32[]{:S(2)}) copy-start(f32[8,16,256]{2,1,0:T(8,128)} %copy-done.2) | copy-start | bytes 393220
  153.5 53.3 %collective-permute-start.15 = (f32[4,1,128]{2,1,0:T(1,128)}, f32[4,1,128]{2,1,0:T(1,128)}, u32[]{:S(2)}, u32[]{:S(2)}) collective-permute-start(f32[4,1,128]{2,1,0:T(1,128)} %slice.387), channel_id=1, source_target_pairs={{0,1},{1,2},{2,3},{3,4},{4,5},{5,6},{6,7},{7,8},{8,9},{9,10},{10,1... | collective-permute-start | bytes 6152 | tf_op jit(solution)/shard_map/ppermute | solution.py:14
  172.1 27.9 %collective-permute-start.10 = (f32[8,1,16,256]{3,2,1,0:T(8,128)}, f32[8,1,16,256]{3,2,1,0:T(8,128)}, u32[]{:S(2)}, u32[]{:S(2)}) collective-permute-start(f32[8,1,16,256]{3,2,1,0:T(8,128)} %get-tuple-element.43), channel_id=1, source_target_pairs={{16,0},{32,16},{48,32},{64,48},{80,64},{96,80},{112,96},{128,112},... | collective-permute-start | bytes 393224 | tf_op jit(solution)/shard_map/ppermute | solution.py:27
  173.4 26.6 %collective-permute-start.11 = (f32[8,1,16,256]{3,2,1,0:T(8,128)}, f32[8,1,16,256]{3,2,1,0:T(8,128)}, u32[]{:S(2)}, u32[]{:S(2)}) collective-permute-start(f32[8,1,16,256]{3,2,1,0:T(8,128)} %get-tuple-element.42), channel_id=1, source_target_pairs={{0,16},{16,32},{32,48},{48,64},{64,80},{80,96},{96,112},{112,128},... | collective-permute-start | bytes 393224 | tf_op jit(solution)/shard_map/ppermute | solution.py:25
  201.2 7.0 %collective-permute-start.12 = (f32[8,10,1,256]{3,0,2,1:T(8,128)S(1)}, f32[8,10,1,256]{3,0,2,1:T(8,128)S(1)}, u32[]{:S(2)}, u32[]{:S(2)}) collective-permute-start(f32[8,10,1,256]{3,0,2,1:T(8,128)S(1)} %copy.442), channel_id=1, source_target_pairs={{1,0},{2,1},{3,2},{4,3},{5,4},{6,5},{7,6},{8,7},{9,8},{10,9},{11,1... | collective-permute-start | bytes 245768 | tf_op jit(solution)/shard_map/ppermute | solution.py:27
  204.3 4.1 collective-permute-start.13
  237.0 31.6 %copy-start.10 = (f32[8,4,8,128]{3,2,1,0:T(8,128)S(1)}, f32[8,4,8,128]{3,2,1,0:T(8,128)}, u32[]{:S(2)}) copy-start(f32[8,4,8,128]{3,2,1,0:T(8,128)} %copy.447) | copy-start | bytes 393220
  237.0 31.6 %copy-start.22 = (f32[4,8,128]{2,1,0:T(8,128)S(1)}, f32[4,8,128]{2,1,0:T(8,128)}, u32[]{:S(2)}) copy-start(f32[4,8,128]{2,1,0:T(8,128)} %copy-done.20) | copy-start | bytes 49156
  237.0 31.6 %copy-start.24 = (f32[4,8,128]{2,1,0:T(8,128)S(1)}, f32[4,8,128]{2,1,0:T(8,128)}, u32[]{:S(2)}) copy-start(f32[4,8,128]{2,1,0:T(8,128)} %slice_reduce_fusion) | copy-start | bytes 49156
  237.0 31.6 %copy-start.29 = (f32[4,8,128]{2,1,0:T(8,128)S(1)}, f32[4,8,128]{2,1,0:T(8,128)}, u32[]{:S(2)}) copy-start(f32[4,8,128]{2,1,0:T(8,128)} %get-tuple-element.24) | copy-start | bytes 49156
  237.0 31.6 %copy-start.30 = (f32[4,8,128]{2,1,0:T(8,128)S(1)}, f32[4,8,128]{2,1,0:T(8,128)}, u32[]{:S(2)}) copy-start(f32[4,8,128]{2,1,0:T(8,128)} %get-tuple-element.25) | copy-start | bytes 49156
  237.0 31.6 %copy-start.31 = (f32[4,8,128]{2,1,0:T(8,128)S(1)}, f32[4,8,128]{2,1,0:T(8,128)}, u32[]{:S(2)}) copy-start(f32[4,8,128]{2,1,0:T(8,128)} %get-tuple-element.62) | copy-start | bytes 49156
  237.1 31.6 %copy-start.32 = (f32[4,8,128]{2,1,0:T(8,128)S(1)}, f32[4,8,128]{2,1,0:T(8,128)}, u32[]{:S(2)}) copy-start(f32[4,8,128]{2,1,0:T(8,128)} %get-tuple-element.63) | copy-start | bytes 49156
  238.1 5.3 %collective-permute-start.16 = (f32[8,1,8,128]{3,2,1,0:T(8,128)S(1)}, f32[8,1,8,128]{3,2,1,0:T(8,128)S(1)}, u32[]{:S(2)}, u32[]{:S(2)}) collective-permute-start(f32[8,1,8,128]{3,2,1,0:T(8,128)S(1)} %get-tuple-element.59), channel_id=1, source_target_pairs={{16,0},{32,16},{48,32},{64,48},{80,64},{96,80},{112,96},{128,112},... | collective-permute-start | bytes 98312 | tf_op jit(solution)/shard_map/ppermute | solution.py:27
  239.4 5.0 %collective-permute-start.17 = (f32[8,1,8,128]{3,2,1,0:T(8,128)S(1)}, f32[8,1,8,128]{3,2,1,0:T(8,128)S(1)}, u32[]{:S(2)}, u32[]{:S(2)}) collective-permute-start(f32[8,1,8,128]{3,2,1,0:T(8,128)S(1)} %get-tuple-element.58), channel_id=1, source_target_pairs={{0,16},{16,32},{32,48},{48,64},{64,80},{80,96},{96,112},{112,128},... | collective-permute-start | bytes 98312 | tf_op jit(solution)/shard_map/ppermute | solution.py:25
  244.4 7.3 %collective-permute-start.18 = (f32[8,6,1,128]{3,2,1,0:T(1,128)S(1)}, f32[8,6,1,128]{3,2,1,0:T(1,128)S(1)}, u32[]{:S(2)}, u32[]{:S(2)}) collective-permute-start(f32[8,6,1,128]{3,2,1,0:T(1,128)S(1)} %get-tuple-element.52), channel_id=1, source_target_pairs={{1,0},{2,1},{3,2},{4,3},{5,4},{6,5},{7,6},{8,7},{9,8},{10,9},{11,1... | collective-permute-start | bytes 73736 | tf_op jit(solution)/shard_map/ppermute | solution.py:27
  247.4 5.3 %collective-permute-start.19 = (f32[8,6,1,128]{3,2,1,0:T(1,128)S(1)}, f32[8,6,1,128]{3,2,1,0:T(1,128)S(1)}, u32[]{:S(2)}, u32[]{:S(2)}) collective-permute-start(f32[8,6,1,128]{3,2,1,0:T(1,128)S(1)} %get-tuple-element.53), channel_id=1, source_target_pairs={{0,1},{1,2},{2,3},{3,4},{4,5},{5,6},{6,7},{7,8},{8,9},{9,10},{10,1... | collective-permute-start | bytes 73736 | tf_op jit(solution)/shard_map/ppermute | solution.py:25
  253.8 5.9 %collective-permute-start.20 = (f32[8,1,8,128]{3,2,1,0:T(8,128)S(1)}, f32[8,1,8,128]{3,2,1,0:T(8,128)S(1)}, u32[]{:S(2)}, u32[]{:S(2)}) collective-permute-start(f32[8,1,8,128]{3,2,1,0:T(8,128)S(1)} %get-tuple-element.57), channel_id=1, source_target_pairs={{16,0},{32,16},{48,32},{64,48},{80,64},{96,80},{112,96},{128,112},... | collective-permute-start | bytes 98312 | tf_op jit(solution)/shard_map/ppermute | solution.py:27
  255.1 5.6 %collective-permute-start.21 = (f32[8,1,8,128]{3,2,1,0:T(8,128)S(1)}, f32[8,1,8,128]{3,2,1,0:T(8,128)S(1)}, u32[]{:S(2)}, u32[]{:S(2)}) collective-permute-start(f32[8,1,8,128]{3,2,1,0:T(8,128)S(1)} %get-tuple-element.56), channel_id=1, source_target_pairs={{0,16},{16,32},{32,48},{48,64},{64,80},{80,96},{96,112},{112,128},... | collective-permute-start | bytes 98312 | tf_op jit(solution)/shard_map/ppermute | solution.py:25
  260.7 7.0 %collective-permute-start.22 = (f32[8,6,1,128]{3,2,1,0:T(1,128)S(1)}, f32[8,6,1,128]{3,2,1,0:T(1,128)S(1)}, u32[]{:S(2)}, u32[]{:S(2)}) collective-permute-start(f32[8,6,1,128]{3,2,1,0:T(1,128)S(1)} %get-tuple-element.50), channel_id=1, source_target_pairs={{1,0},{2,1},{3,2},{4,3},{5,4},{6,5},{7,6},{8,7},{9,8},{10,9},{11,1... | collective-permute-start | bytes 73736 | tf_op jit(solution)/shard_map/ppermute | solution.py:27
  262.6 6.0 %collective-permute-start.23 = (f32[8,6,1,128]{3,2,1,0:T(1,128)S(1)}, f32[8,6,1,128]{3,2,1,0:T(1,128)S(1)}, u32[]{:S(2)}, u32[]{:S(2)}) collective-permute-start(f32[8,6,1,128]{3,2,1,0:T(1,128)S(1)} %get-tuple-element.51), channel_id=1, source_target_pairs={{0,1},{1,2},{2,3},{3,4},{4,5},{5,6},{6,7},{7,8},{8,9},{9,10},{10,1... | collective-permute-start | bytes 73736 | tf_op jit(solution)/shard_map/ppermute | solution.py:25
  268.8 5.9 %collective-permute-start.24 = (f32[8,1,8,128]{3,2,1,0:T(8,128)S(1)}, f32[8,1,8,128]{3,2,1,0:T(8,128)S(1)}, u32[]{:S(2)}, u32[]{:S(2)}) collective-permute-start(f32[8,1,8,128]{3,2,1,0:T(8,128)S(1)} %get-tuple-element.55), channel_id=1, source_target_pairs={{16,0},{32,16},{48,32},{64,48},{80,64},{96,80},{112,96},{128,112},... | collective-permute-start | bytes 98312 | tf_op jit(solution)/shard_map/ppermute | solution.py:27
  270.1 5.6 %collective-permute-start.25 = (f32[8,1,8,128]{3,2,1,0:T(8,128)S(1)}, f32[8,1,8,128]{3,2,1,0:T(8,128)S(1)}, u32[]{:S(2)}, u32[]{:S(2)}) collective-permute-start(f32[8,1,8,128]{3,2,1,0:T(8,128)S(1)} %get-tuple-element.54), channel_id=1, source_target_pairs={{0,16},{16,32},{32,48},{48,64},{64,80},{80,96},{96,112},{112,128},... | collective-permute-start | bytes 98312 | tf_op jit(solution)/shard_map/ppermute | solution.py:25
  275.8 7.0 %collective-permute-start.26 = (f32[8,6,1,128]{3,2,1,0:T(1,128)S(1)}, f32[8,6,1,128]{3,2,1,0:T(1,128)S(1)}, u32[]{:S(2)}, u32[]{:S(2)}) collective-permute-start(f32[8,6,1,128]{3,2,1,0:T(1,128)S(1)} %get-tuple-element.48), channel_id=1, source_target_pairs={{1,0},{2,1},{3,2},{4,3},{5,4},{6,5},{7,6},{8,7},{9,8},{10,9},{11,1... | collective-permute-start | bytes 73736 | tf_op jit(solution)/shard_map/ppermute | solution.py:27
  277.7 6.0 %collective-permute-start.27 = (f32[8,6,1,128]{3,2,1,0:T(1,128)S(1)}, f32[8,6,1,128]{3,2,1,0:T(1,128)S(1)}, u32[]{:S(2)}, u32[]{:S(2)}) collective-permute-start(f32[8,6,1,128]{3,2,1,0:T(1,128)S(1)} %get-tuple-element.49), channel_id=1, source_target_pairs={{0,1},{1,2},{2,3},{3,4},{4,5},{5,6},{6,7},{7,8},{8,9},{9,10},{10,1... | collective-permute-start | bytes 73736 | tf_op jit(solution)/shard_map/ppermute | solution.py:25
  306.5 16.7 %copy-start.7 = (f32[8,16,256]{2,1,0:T(8,128)S(1)}, f32[8,16,256]{2,1,0:T(8,128)}, u32[]{:S(2)}) copy-start(f32[8,16,256]{2,1,0:T(8,128)} %get-tuple-element.28) | copy-start | bytes 393220
  306.6 16.7 %copy-start.9 = (f32[8,16,256]{2,1,0:T(8,128)S(1)}, f32[8,16,256]{2,1,0:T(8,128)}, u32[]{:S(2)}) copy-start(f32[8,16,256]{2,1,0:T(8,128)} %copy-done.8) | copy-start | bytes 393220
  306.6 16.7 %copy-start.13 = (f32[8,16,256]{2,1,0:T(8,128)S(1)}, f32[8,16,256]{2,1,0:T(8,128)}, u32[]{:S(2)}) copy-start(f32[8,16,256]{2,1,0:T(8,128)} %copy-done.11) | copy-start | bytes 393220
  306.6 16.7 %copy-start.16 = (f32[8,16,256]{2,1,0:T(8,128)S(1)}, f32[8,16,256]{2,1,0:T(8,128)}, u32[]{:S(2)}) copy-start(f32[8,16,256]{2,1,0:T(8,128)} %copy-done.14) | copy-start | bytes 393220
  306.6 16.7 %copy-start.19 = (f32[8,16,256]{2,1,0:T(8,128)S(1)}, f32[8,16,256]{2,1,0:T(8,128)}, u32[]{:S(2)}) copy-start(f32[8,16,256]{2,1,0:T(8,128)} %copy-done.17) | copy-start | bytes 393220
  306.6 6.5 %collective-permute-start.28 = (f32[8,1,16,256]{3,2,1,0:T(8,128)S(1)}, f32[8,1,16,256]{3,2,1,0:T(8,128)S(1)}, u32[]{:S(2)}, u32[]{:S(2)}) collective-permute-start(f32[8,1,16,256]{3,2,1,0:T(8,128)S(1)} %get-tuple-element.41), channel_id=1, source_target_pairs={{16,0},{32,16},{48,32},{64,48},{80,64},{96,80},{112,96},{128,112},... | collective-permute-start | bytes 393224 | tf_op jit(solution)/shard_map/ppermute | solution.py:27
  308.1 6.5 %collective-permute-start.29 = (f32[8,1,16,256]{3,2,1,0:T(8,128)S(1)}, f32[8,1,16,256]{3,2,1,0:T(8,128)S(1)}, u32[]{:S(2)}, u32[]{:S(2)}) collective-permute-start(f32[8,1,16,256]{3,2,1,0:T(8,128)S(1)} %get-tuple-element.40), channel_id=1, source_target_pairs={{0,16},{16,32},{32,48},{48,64},{64,80},{80,96},{96,112},{112,128},... | collective-permute-start | bytes 393224 | tf_op jit(solution)/shard_map/ppermute | solution.py:25
  314.7 7.2 %collective-permute-start.30 = (f32[8,10,1,256]{3,0,2,1:T(8,128)S(1)}, f32[8,10,1,256]{3,0,2,1:T(8,128)S(1)}, u32[]{:S(2)}, u32[]{:S(2)}) collective-permute-start(f32[8,10,1,256]{3,0,2,1:T(8,128)S(1)} %copy.453), channel_id=1, source_target_pairs={{1,0},{2,1},{3,2},{4,3},{5,4},{6,5},{7,6},{8,7},{9,8},{10,9},{11,1... | collective-permute-start | bytes 245768 | tf_op jit(solution)/shard_map/ppermute | solution.py:27
  316.7 6.5 %collective-permute-start.31 = (f32[8,10,1,256]{3,0,2,1:T(8,128)S(1)}, f32[8,10,1,256]{3,0,2,1:T(8,128)S(1)}, u32[]{:S(2)}, u32[]{:S(2)}) collective-permute-start(f32[8,10,1,256]{3,0,2,1:T(8,128)S(1)} %copy.455), channel_id=1, source_target_pairs={{0,1},{1,2},{2,3},{3,4},{4,5},{5,6},{6,7},{7,8},{8,9},{9,10},{10,1... | collective-permute-start | bytes 245768 | tf_op jit(solution)/shard_map/ppermute | solution.py:25
  (21 other events, 130.1 us)
where the time goes:
time: 429 us; the launch traced here: 427 us
  blocking collectives  176 us (41%)
  starting transfers between devices  98.6 us (23%)
  local copies, waits for them, and re-layouts  80.4 us (19%)
  other arithmetic  57.3 us (13%)
  waiting for transfers between devices  9.35 us (2%)
    psum x1, blocking collectives, per_device(): gram = lax.psum(local_gram, ('gx', 'gy'))  93.9 us
    psum x1, blocking collectives, rayleigh_sums(): lax.psum((jnp.sum(vectors * applied, axis=(1, 2, 3)), jnp.sum(vectors * (...  82.2 us
    ppermute x14, starting transfers between devices, with_halo(): lax.ppermute(tail, axis, [(i, (i + 1) % count) for i in range(ends)])  59 us
    ppermute x14, starting transfers between devices, with_halo(): lax.ppermute(head, axis, [((i + 1) % count, i) for i in range(ends)])  26.2 us
    ppermute x4, starting transfers between devices, shifted(): return lax.ppermute(shard, axis, pairs)  13.3 us
    reduce_sum x1, other arithmetic, restrict(): field.reshape(kk, sx // 2, 2, sy // 2, 2, sz // 2, 2).sum(axis=(2, 4, 6))  13.1 us
    reshape x1, local copies, waits for them, and re-layouts, prolong(): jnp.broadcast_to(field[:, :, None, :, None, :, None], (kk, sx, 2, sy, 2,...  10.6 us
    reshape x1, local copies, waits for them, and re-layouts, coarse_weights(): dsum = degree.reshape(shape).sum(axis=(1, 3, 5))  10.5 us
  transfers between devices with their start and end apart: 32, of which 10 were waited for; matrix products, arithmetic and copies ran while one was open for 17% of the time, Pallas kernels for 0%

commit v1 on v0

--- a/solution.py
+++ b/solution.py
@@ -76,11 +76,14 @@
 
 def rayleigh_sums(vectors, applied, degree):
     return lax.psum(
-        (
-            jnp.sum(vectors * applied, axis=(1, 2, 3)),
-            jnp.sum(vectors * (degree[None] * vectors), axis=(1, 2, 3)),
+        lax.psum(
+            (
+                jnp.sum(vectors * applied, axis=(1, 2, 3)),
+                jnp.sum(vectors * (degree[None] * vectors), axis=(1, 2, 3)),
+            ),
+            "gy",
         ),
-        ("gx", "gy"),
+        "gx",
     )
 
 

time: 429 us -> 411 us (0.958)
  blocking collectives: 176 us -> 152 us
  starting transfers between devices: 98.6 us -> 104 us
    psum x1, blocking collectives: 82.2 us -> 26.8 us  [rayleigh_sums(): lax.psum((jnp.sum(vectors * applied, axis=(1, 2, 3)), jnp.sum(vectors * (...]
    psum x0 -> x1, blocking collectives: none -> 33.1 us  [rayleigh_sums(): lax.psum(lax.psum((jnp.sum(vectors * applied, axis=(1, 2, 3)), jnp.sum(ve...]
    ppermute x14, starting transfers between devices: 26.2 us -> 34 us  [with_halo(): lax.ppermute(head, axis, [((i + 1) % count, i) for i in range(ends)])]
where the time goes in v1:
time: 411 us; the launch traced here: 409 us
  blocking collectives  152 us (37%)
  starting transfers between devices  104 us (25%)
  local copies, waits for them, and re-layouts  80.5 us (20%)
  other arithmetic  57.4 us (14%)
  waiting for transfers between devices  9.34 us (2%)
    psum x1, blocking collectives, per_device(): gram = lax.psum(local_gram, ('gx', 'gy'))  92.2 us
    ppermute x14, starting transfers between devices, with_halo(): lax.ppermute(tail, axis, [(i, (i + 1) % count) for i in range(ends)])  58.2 us
    ppermute x14, starting transfers between devices, with_halo(): lax.ppermute(head, axis, [((i + 1) % count, i) for i in range(ends)])  34 us
    psum x1, blocking collectives, rayleigh_sums(): lax.psum(lax.psum((jnp.sum(vectors * applied, axis=(1, 2, 3)), jnp.sum(ve...  33.1 us
    psum x1, blocking collectives, rayleigh_sums(): lax.psum((jnp.sum(vectors * applied, axis=(1, 2, 3)), jnp.sum(vectors * (...  26.8 us
    reduce_sum x1, other arithmetic, restrict(): field.reshape(kk, sx // 2, 2, sy // 2, 2, sz // 2, 2).sum(axis=(2, 4, 6))  13.1 us
    ppermute x4, starting transfers between devices, shifted(): return lax.ppermute(shard, axis, pairs)  12.2 us
    reshape x1, local copies, waits for them, and re-layouts, prolong(): jnp.broadcast_to(field[:, :, None, :, None, :, None], (kk, sx, 2, sy, 2,...  10.6 us
  transfers between devices with their start and end apart: 32, of which 10 were waited for; matrix products, arithmetic and copies ran while one was open for 17% of the time, Pallas kernels for 0%

profile of v1, /device:TPU:1, one launch (start us, length us, event | category | flops | bytes accessed | tf_op | source)
XLA Modules:
  0.0 409.5 jit_solution(3150823588027034004)
XLA Ops:
  1.7 3.9 collective-permute-start
  6.6 4.4 %collective-permute-start.1 = (f32[8,1,256]{2,1,0:T(1,128)S(1)}, f32[8,1,256]{2,1,0:T(1,128)S(1)}, u32[]{:S(2)}, u32[]{:S(2)}) collective-permute-start(f32[8,1,256]{2,1,0:T(1,128)S(1)} %slice.374), channel_id=1, source_target_pairs={{0,1},{1,2},{2,3},{3,4},{4,5},{5,6},{6,7},{7,8},{8,9},{9,10},{10,1... | collective-permute-start | bytes 24584 | tf_op jit(solution)/shard_map/ppermute | solution.py:14
  12.0 3.1 collective-permute-start.3
  16.5 9.8 %reshape.74 = f32[4,2,8,2,128,2]{5,4,3,2,1,0:T(8,128)} reshape(f32[8,16,256]{2,1,0:T(8,128)S(1)} %broadcast_select_fusion.2) | data formatting | bytes 262144 | tf_op jit(solution)/shard_map/reshape | solution.py:93
  26.6 1.9 collective-permute-start.4
  28.6 3.6 collective-permute-start.5
  33.8 2.1 fusion
  35.9 26.8 %all-reduce.9 = (f32[8]{0:T(128)S(1)}, f32[8]{0:T(128)S(1)}) all-reduce(f32[8]{0:T(128)S(1)} %get-tuple-element.19, f32[8]{0:T(128)S(1)} %get-tuple-element.18), channel_id=1, replica_groups=mesh['gx'=16,'gy'=16] {'gy'}, use_global_device_ids=true, to_apply=%region_1.2 | all-reduce | flops 16 | bytes 128 | tf_op jit(solution)/shard_map/psum | solution.py:79
  62.7 33.1 %all-reduce.10 = (f32[8]{0:T(128)S(1)}, f32[8]{0:T(128)S(1)}) all-reduce(f32[8]{0:T(128)S(1)} %get-tuple-element.20, f32[8]{0:T(128)S(1)} %get-tuple-element.21), channel_id=1, replica_groups=mesh['gx'=16,'gy'=16] {'gx'}, use_global_device_ids=true, to_apply=%region_2.3 | all-reduce | flops 16 | bytes 128 | tf_op jit(solution)/shard_map/psum | solution.py:78
  95.8 1.7 multiply_divide_fusion
  99.5 4.6 %collective-permute-start.7 = (f32[8,1,16,256]{3,2,1,0:T(8,128)}, f32[8,1,16,256]{3,2,1,0:T(8,128)}, u32[]{:S(2)}, u32[]{:S(2)}) collective-permute-start(f32[8,1,16,256]{3,2,1,0:T(8,128)} %get-tuple-element.46), channel_id=1, source_target_pairs={{0,16},{16,32},{32,48},{48,64},{64,80},{80,96},{96,112},{112,128},... | collective-permute-start | bytes 393224 | tf_op jit(solution)/shard_map/ppermute | solution.py:25
  104.2 2.8 slice_reduce_fusion.2
  108.2 1.9 collective-permute-start.14
  110.1 9.8 %reshape.75 = f32[4,2,8,2,128,2]{5,4,3,2,1,0:T(8,128)} reshape(f32[8,16,256]{2,1,0:T(8,128)S(1)} %broadcast_select_fusion.1) | data formatting | bytes 262144 | tf_op jit(solution)/shard_map/reshape | solution.py:94
  120.9 10.2 %collective-permute-start.8 = (f32[8,10,1,256]{3,0,2,1:T(8,128)S(1)}, f32[8,10,1,256]{3,0,2,1:T(8,128)S(1)}, u32[]{:S(2)}, u32[]{:S(2)}) collective-permute-start(f32[8,10,1,256]{3,0,2,1:T(8,128)S(1)} %copy.438), channel_id=1, source_target_pairs={{1,0},{2,1},{3,2},{4,3},{5,4},{6,5},{7,6},{8,7},{9,8},{10,9},{11,1... | collective-permute-start | bytes 245768 | tf_op jit(solution)/shard_map/ppermute | solution.py:27
  131.1 1.9 collective-permute-start.9
  133.0 2.8 slice_reduce_fusion.1
  136.5 2.0 collective-permute-start.15
  138.5 9.8 %reshape.76 = f32[4,2,8,2,128,2]{5,4,3,2,1,0:T(8,128)} reshape(f32[8,16,256]{2,1,0:T(8,128)S(1)} %broadcast_select_fusion) | data formatting | bytes 262144 | tf_op jit(solution)/shard_map/reshape | solution.py:95
  148.5 5.3 %fusion.13 = f32[8,8,16,256]{3,2,1,0:T(8,128)S(1)} fusion(f32[8,8,16,256]{3,2,1,0:T(8,128)} %copy-done.1, f32[8,8,16,256]{3,2,1,0:T(8,128)S(1)} %get-tuple-element.29, f32[8,10,1,256]{3,2,1,0:T(1,128)S(1)} %copy.441, f32[8,1,16,256]{3,2,1,0:T(8,128)} %copy-done.25, f32[8,1,16,256]{3,2,1,0:T(8,128)} %collective-permute-done.7, ...), kind=kLoop, calls=%fused_computation.28 | loop fusion | flops 6553600 | bytes 4489216 | tf_op jit(solution)/shard_map/add | solution.py:72
  155.8 4.6 %collective-permute-start.11 = (f32[8,1,16,256]{3,2,1,0:T(8,128)}, f32[8,1,16,256]{3,2,1,0:T(8,128)}, u32[]{:S(2)}, u32[]{:S(2)}) collective-permute-start(f32[8,1,16,256]{3,2,1,0:T(8,128)} %get-tuple-element.44), channel_id=1, source_target_pairs={{0,16},{16,32},{32,48},{48,64},{64,80},{80,96},{96,112},{112,128},... | collective-permute-start | bytes 393224 | tf_op jit(solution)/shard_map/ppermute | solution.py:25
  160.5 6.8 %slice_reduce_fusion = f32[4,8,128]{2,1,0:T(8,128)} fusion(f32[4,2,8,2,128,2]{5,4,3,2,1,0:T(8,128)} %reshape.76), kind=kLoop, calls=%fused_computation | loop fusion | flops 12288 | bytes 81920 | tf_op jit(solution)/shard_map/reduce_sum | solution.py:95
  167.3 10.5 %reshape.77 = f32[4,2,8,2,128,2]{5,4,3,2,1,0:T(8,128)} reshape(f32[8,16,256]{2,1,0:T(8,128)} %copy-done.8) | data formatting | bytes 262144 | tf_op jit(solution)/shard_map/reshape | solution.py:96
  177.8 4.6 %reduce_sum.69 = f32[4,8,128]{2,1,0:T(8,128)} reduce(f32[4,2,8,2,128,2]{5,4,3,2,1,0:T(8,128)} %reshape.77, f32[]{:T(128)} %constant.65.clone.1), dimensions={1,3,5}, to_apply=%region_10.11 | reduce | flops 28672 | bytes 147460 | tf_op jit(solution)/shard_map/reduce_sum | solution.py:96
  183.7 3.5 collective-permute-start.12
  187.2 2.0 collective-permute-start.13
  190.9 2.8 fusion.19
  193.8 9.8 %copy.446 = f32[8,8,16,256]{0,3,2,1:T(8,128)} copy(f32[8,8,16,256]{3,2,1,0:T(8,128)} %fusion.19) | data formatting | bytes 2097152 | tf_op jit(solution)/shard_map/sub | solution.py:131
  203.6 13.1 %reduce_sum.65 = f32[8,4,8,128]{0,3,2,1:T(8,128)} reduce(f32[8,4,2,8,2,128,2]{0,6,5,4,3,2,1:T(2,128)} %bitcast.30, f32[]{:T(128)} %constant.65.clone.1), dimensions={2,4,6}, to_apply=%region_6.7 | reduce | flops 229376 | bytes 1179652 | tf_op jit(solution)/shard_map/reduce_sum | solution.py:102
  216.7 2.8 copy.447
  221.9 4.0 collective-permute-start.17
  226.9 3.4 collective-permute-start.18
  230.4 3.8 collective-permute-start.19
  237.6 4.6 %collective-permute-start.21 = (f32[8,1,8,128]{3,2,1,0:T(8,128)S(1)}, f32[8,1,8,128]{3,2,1,0:T(8,128)S(1)}, u32[]{:S(2)}, u32[]{:S(2)}) collective-permute-start(f32[8,1,8,128]{3,2,1,0:T(8,128)S(1)} %get-tuple-element.58), channel_id=1, source_target_pairs={{0,16},{16,32},{32,48},{48,64},{64,80},{80,96},{96,112},{112,128},... | collective-permute-start | bytes 98312 | tf_op jit(solution)/shard_map/ppermute | solution.py:25
  243.2 1.9 collective-permute-start.22
  245.1 5.1 %collective-permute-start.23 = (f32[8,6,1,128]{3,2,1,0:T(1,128)S(1)}, f32[8,6,1,128]{3,2,1,0:T(1,128)S(1)}, u32[]{:S(2)}, u32[]{:S(2)}) collective-permute-start(f32[8,6,1,128]{3,2,1,0:T(1,128)S(1)} %get-tuple-element.53), channel_id=1, source_target_pairs={{0,1},{1,2},{2,3},{3,4},{4,5},{5,6},{6,7},{7,8},{8,9},{9,10},{10,1... | collective-permute-start | bytes 73736 | tf_op jit(solution)/shard_map/ppermute | solution.py:25
  252.7 4.7 %collective-permute-start.25 = (f32[8,1,8,128]{3,2,1,0:T(8,128)S(1)}, f32[8,1,8,128]{3,2,1,0:T(8,128)S(1)}, u32[]{:S(2)}, u32[]{:S(2)}) collective-permute-start(f32[8,1,8,128]{3,2,1,0:T(8,128)S(1)} %get-tuple-element.56), channel_id=1, source_target_pairs={{0,16},{16,32},{32,48},{48,64},{64,80},{80,96},{96,112},{112,128},... | collective-permute-start | bytes 98312 | tf_op jit(solution)/shard_map/ppermute | solution.py:25
  258.5 1.9 collective-permute-start.26
  260.4 5.1 %collective-permute-start.27 = (f32[8,6,1,128]{3,2,1,0:T(1,128)S(1)}, f32[8,6,1,128]{3,2,1,0:T(1,128)S(1)}, u32[]{:S(2)}, u32[]{:S(2)}) collective-permute-start(f32[8,6,1,128]{3,2,1,0:T(1,128)S(1)} %get-tuple-element.51), channel_id=1, source_target_pairs={{0,1},{1,2},{2,3},{3,4},{4,5},{5,6},{6,7},{7,8},{8,9},{9,10},{10,1... | collective-permute-start | bytes 73736 | tf_op jit(solution)/shard_map/ppermute | solution.py:25
  267.2 2.9 copy.451
  270.1 7.1 %broadcast_in_dim.30 = f32[8,4,2,8,2,128,2]{0,6,5,4,3,2,1:T(2,128)} broadcast(f32[8,4,8,128]{0,3,2,1:T(8,128)} %copy.451), dimensions={0,1,3,5} | broadcast | bytes 1179648 | tf_op jit(solution)/shard_map/broadcast_in_dim | solution.py:107
  277.2 10.6 %copy.452 = f32[8,8,16,256]{3,2,1,0:T(8,128)} copy(f32[8,8,16,256]{0,3,2,1:T(8,128)} %bitcast.31) | data formatting | bytes 2097152 | tf_op jit(solution)/shard_map/reshape | solution.py:107
  290.8 4.6 %collective-permute-start.29 = (f32[8,1,16,256]{3,2,1,0:T(8,128)S(1)}, f32[8,1,16,256]{3,2,1,0:T(8,128)S(1)}, u32[]{:S(2)}, u32[]{:S(2)}) collective-permute-start(f32[8,1,16,256]{3,2,1,0:T(8,128)S(1)} %get-tuple-element.42), channel_id=1, source_target_pairs={{0,16},{16,32},{32,48},{48,64},{64,80},{80,96},{96,112},{112,128},... | collective-permute-start | bytes 393224 | tf_op jit(solution)/shard_map/ppermute | solution.py:25
  297.4 1.9 collective-permute-start.30
  299.3 6.3 %collective-permute-start.31 = (f32[8,10,1,256]{3,0,2,1:T(8,128)S(1)}, f32[8,10,1,256]{3,0,2,1:T(8,128)S(1)}, u32[]{:S(2)}, u32[]{:S(2)}) collective-permute-start(f32[8,10,1,256]{3,0,2,1:T(8,128)S(1)} %copy.455), channel_id=1, source_target_pairs={{0,1},{1,2},{2,3},{3,4},{4,5},{5,6},{6,7},{7,8},{8,9},{9,10},{10,1... | collective-permute-start | bytes 245768 | tf_op jit(solution)/shard_map/ppermute | solution.py:25
  307.0 1.6 broadcast_multiply_fusion
  308.6 3.0 convolution_bitcast_fusion
  311.6 92.2 %psum.39 = f32[8,8]{0,1:T(8,128)S(1)} all-reduce(f32[8,8]{0,1:T(8,128)S(1)} %convolution_bitcast_fusion), channel_id=1, replica_groups=mesh['gx'=16,'gy'=16] {'gx','gy'}, use_global_device_ids=true, to_apply=%region_11.12 | all-reduce | flops 64 | bytes 512 | tf_op jit(solution)/shard_map/psum | solution.py:145
  (175 shorter events, 40.7 us)
Async XLA Ops:
  1.6 24.6 %copy-start.2 = (f32[8,16,256]{2,1,0:T(8,128)}, f32[8,16,256]{2,1,0:T(8,128)S(1)}, u32[]{:S(2)}) copy-start(f32[8,16,256]{2,1,0:T(8,128)S(1)} %broadcast_select_fusion.2) | copy-start | bytes 393220
  1.7 30.6 %collective-permute-start = (f32[1,16,256]{2,1,0:T(8,128)S(1)}, f32[1,16,256]{2,1,0:T(8,128)S(1)}, u32[]{:S(2)}, u32[]{:S(2)}) collective-permute-start(f32[1,16,256]{2,1,0:T(8,128)S(1)} %slice.372), channel_id=1, source_target_pairs={{0,16},{16,32},{32,48},{48,64},{64,80},{80,96},{96,112},{112,128},... | collective-permute-start | bytes 49160 | tf_op jit(solution)/shard_map/ppermute | solution.py:14
  6.6 25.6 %collective-permute-start.1 = (f32[8,1,256]{2,1,0:T(1,128)S(1)}, f32[8,1,256]{2,1,0:T(1,128)S(1)}, u32[]{:S(2)}, u32[]{:S(2)}) collective-permute-start(f32[8,1,256]{2,1,0:T(1,128)S(1)} %slice.374), channel_id=1, source_target_pairs={{0,1},{1,2},{2,3},{3,4},{4,5},{5,6},{6,7},{7,8},{8,9},{9,10},{10,1... | collective-permute-start | bytes 24584 | tf_op jit(solution)/shard_map/ppermute | solution.py:14
  12.0 14.3 %collective-permute-start.3 = (f32[8,1,16,256]{3,2,1,0:T(8,128)S(1)}, f32[8,1,16,256]{3,2,1,0:T(8,128)S(1)}, u32[]{:S(2)}, u32[]{:S(2)}) collective-permute-start(f32[8,1,16,256]{3,2,1,0:T(8,128)S(1)} %get-tuple-element.49), channel_id=1, source_target_pairs={{0,16},{16,32},{32,48},{48,64},{64,80},{80,96},{96,112},{112,128},... | collective-permute-start | bytes 393224 | tf_op jit(solution)/shard_map/ppermute | solution.py:25
  15.2 11.3 %collective-permute-start.2 = (f32[8,1,16,256]{3,2,1,0:T(8,128)S(1)}, f32[8,1,16,256]{3,2,1,0:T(8,128)S(1)}, u32[]{:S(2)}, u32[]{:S(2)}) collective-permute-start(f32[8,1,16,256]{3,2,1,0:T(8,128)S(1)} %get-tuple-element.48), channel_id=1, source_target_pairs={{16,0},{32,16},{48,32},{64,48},{80,64},{96,80},{112,96},{128,112},... | collective-permute-start | bytes 393224 | tf_op jit(solution)/shard_map/ppermute | solution.py:27
  26.6 6.5 %collective-permute-start.4 = (f32[8,10,1,256]{3,0,2,1:T(8,128)S(1)}, f32[8,10,1,256]{3,0,2,1:T(8,128)S(1)}, u32[]{:S(2)}, u32[]{:S(2)}) collective-permute-start(f32[8,10,1,256]{3,0,2,1:T(8,128)S(1)} %copy.466), channel_id=1, source_target_pairs={{1,0},{2,1},{3,2},{4,3},{5,4},{6,5},{7,6},{8,7},{9,8},{10,9},{11,1... | collective-permute-start | bytes 245768 | tf_op jit(solution)/shard_map/ppermute | solution.py:27
  28.6 5.1 %collective-permute-start.5 = (f32[8,10,1,256]{3,0,2,1:T(8,128)S(1)}, f32[8,10,1,256]{3,0,2,1:T(8,128)S(1)}, u32[]{:S(2)}, u32[]{:S(2)}) collective-permute-start(f32[8,10,1,256]{3,0,2,1:T(8,128)S(1)} %copy.467), channel_id=1, source_target_pairs={{0,1},{1,2},{2,3},{3,4},{4,5},{5,6},{6,7},{7,8},{8,9},{9,10},{10,1... | collective-permute-start | bytes 245768 | tf_op jit(solution)/shard_map/ppermute | solution.py:25
  33.8 62.0 %copy-start.5 = (f32[8,16,256]{2,1,0:T(8,128)S(1)}, f32[8,16,256]{2,1,0:T(8,128)}, u32[]{:S(2)}) copy-start(f32[8,16,256]{2,1,0:T(8,128)} %get-tuple-element.30) | copy-start | bytes 393220
  97.5 22.3 %copy-start.1 = (f32[8,8,16,256]{3,2,1,0:T(8,128)}, f32[8,8,16,256]{3,2,1,0:T(8,128)S(1)}, u32[]{:S(2)}) copy-start(f32[8,8,16,256]{3,2,1,0:T(8,128)S(1)} %get-tuple-element.28) | copy-start | bytes 3145732
  98.2 21.6 %collective-permute-start.6 = (f32[8,1,16,256]{3,2,1,0:T(8,128)}, f32[8,1,16,256]{3,2,1,0:T(8,128)S(1)}, u32[]{:S(2)}, u32[]{:S(2)}) collective-permute-start(f32[8,1,16,256]{3,2,1,0:T(8,128)} %get-tuple-element.47), channel_id=1, source_target_pairs={{16,0},{32,16},{48,32},{64,48},{80,64},{96,80},{112,96},{128,112},... | collective-permute-start | bytes 393224 | tf_op jit(solution)/shard_map/ppermute | solution.py:27
  99.5 20.3 %collective-permute-start.7 = (f32[8,1,16,256]{3,2,1,0:T(8,128)}, f32[8,1,16,256]{3,2,1,0:T(8,128)}, u32[]{:S(2)}, u32[]{:S(2)}) collective-permute-start(f32[8,1,16,256]{3,2,1,0:T(8,128)} %get-tuple-element.46), channel_id=1, source_target_pairs={{0,16},{16,32},{32,48},{48,64},{64,80},{80,96},{96,112},{112,128},... | collective-permute-start | bytes 393224 | tf_op jit(solution)/shard_map/ppermute | solution.py:25
  108.2 81.1 %collective-permute-start.14 = (f32[1,8,128]{2,1,0:T(8,128)}, f32[1,8,128]{2,1,0:T(8,128)}, u32[]{:S(2)}, u32[]{:S(2)}) collective-permute-start(f32[1,8,128]{2,1,0:T(8,128)} %slice.384), channel_id=1, source_target_pairs={{0,16},{16,32},{32,48},{48,64},{64,80},{80,96},{96,112},{112,128},... | collective-permute-start | bytes 12296 | tf_op jit(solution)/shard_map/ppermute | solution.py:14
  119.8 16.0 %copy-start.25 = (f32[8,1,16,256]{3,2,1,0:T(8,128)}, f32[8,1,16,256]{3,2,1,0:T(8,128)S(1)}, u32[]{:S(2)}) copy-start(f32[8,1,16,256]{3,2,1,0:T(8,128)S(1)} %collective-permute-done.6) | copy-start | bytes 393220
  120.9 27.4 %collective-permute-start.8 = (f32[8,10,1,256]{3,0,2,1:T(8,128)S(1)}, f32[8,10,1,256]{3,0,2,1:T(8,128)S(1)}, u32[]{:S(2)}, u32[]{:S(2)}) collective-permute-start(f32[8,10,1,256]{3,0,2,1:T(8,128)S(1)} %copy.438), channel_id=1, source_target_pairs={{1,0},{2,1},{3,2},{4,3},{5,4},{6,5},{7,6},{8,7},{9,8},{10,9},{11,1... | collective-permute-start | bytes 245768 | tf_op jit(solution)/shard_map/ppermute | solution.py:27
  131.1 17.3 %collective-permute-start.9 = (f32[8,10,1,256]{3,0,2,1:T(8,128)S(1)}, f32[8,10,1,256]{3,0,2,1:T(8,128)S(1)}, u32[]{:S(2)}, u32[]{:S(2)}) collective-permute-start(f32[8,10,1,256]{3,0,2,1:T(8,128)S(1)} %copy.440), channel_id=1, source_target_pairs={{0,1},{1,2},{2,3},{3,4},{4,5},{5,6},{6,7},{7,8},{8,9},{9,10},{10,1... | collective-permute-start | bytes 245768 | tf_op jit(solution)/shard_map/ppermute | solution.py:25
  136.5 52.8 %collective-permute-start.15 = (f32[4,1,128]{2,1,0:T(1,128)}, f32[4,1,128]{2,1,0:T(1,128)}, u32[]{:S(2)}, u32[]{:S(2)}) collective-permute-start(f32[4,1,128]{2,1,0:T(1,128)} %slice.387), channel_id=1, source_target_pairs={{0,1},{1,2},{2,3},{3,4},{4,5},{5,6},{6,7},{7,8},{8,9},{9,10},{10,1... | collective-permute-start | bytes 6152 | tf_op jit(solution)/shard_map/ppermute | solution.py:14
  154.6 27.9 %collective-permute-start.10 = (f32[8,1,16,256]{3,2,1,0:T(8,128)}, f32[8,1,16,256]{3,2,1,0:T(8,128)}, u32[]{:S(2)}, u32[]{:S(2)}) collective-permute-start(f32[8,1,16,256]{3,2,1,0:T(8,128)} %get-tuple-element.45), channel_id=1, source_target_pairs={{16,0},{32,16},{48,32},{64,48},{80,64},{96,80},{112,96},{128,112},... | collective-permute-start | bytes 393224 | tf_op jit(solution)/shard_map/ppermute | solution.py:27
  155.8 26.6 %collective-permute-start.11 = (f32[8,1,16,256]{3,2,1,0:T(8,128)}, f32[8,1,16,256]{3,2,1,0:T(8,128)}, u32[]{:S(2)}, u32[]{:S(2)}) collective-permute-start(f32[8,1,16,256]{3,2,1,0:T(8,128)} %get-tuple-element.44), channel_id=1, source_target_pairs={{0,16},{16,32},{32,48},{48,64},{64,80},{80,96},{96,112},{112,128},... | collective-permute-start | bytes 393224 | tf_op jit(solution)/shard_map/ppermute | solution.py:25
  183.7 7.0 %collective-permute-start.12 = (f32[8,10,1,256]{3,0,2,1:T(8,128)S(1)}, f32[8,10,1,256]{3,0,2,1:T(8,128)S(1)}, u32[]{:S(2)}, u32[]{:S(2)}) collective-permute-start(f32[8,10,1,256]{3,0,2,1:T(8,128)S(1)} %copy.442), channel_id=1, source_target_pairs={{1,0},{2,1},{3,2},{4,3},{5,4},{6,5},{7,6},{8,7},{9,8},{10,9},{11,1... | collective-permute-start | bytes 245768 | tf_op jit(solution)/shard_map/ppermute | solution.py:27
  187.2 3.6 collective-permute-start.13
  219.5 31.6 %copy-start.10 = (f32[8,4,8,128]{3,2,1,0:T(8,128)S(1)}, f32[8,4,8,128]{3,2,1,0:T(8,128)}, u32[]{:S(2)}) copy-start(f32[8,4,8,128]{3,2,1,0:T(8,128)} %copy.447) | copy-start | bytes 393220
  219.5 31.6 %copy-start.22 = (f32[4,8,128]{2,1,0:T(8,128)S(1)}, f32[4,8,128]{2,1,0:T(8,128)}, u32[]{:S(2)}) copy-start(f32[4,8,128]{2,1,0:T(8,128)} %copy-done.20) | copy-start | bytes 49156
  219.5 31.6 %copy-start.24 = (f32[4,8,128]{2,1,0:T(8,128)S(1)}, f32[4,8,128]{2,1,0:T(8,128)}, u32[]{:S(2)}) copy-start(f32[4,8,128]{2,1,0:T(8,128)} %slice_reduce_fusion) | copy-start | bytes 49156
  219.5 31.6 %copy-start.29 = (f32[4,8,128]{2,1,0:T(8,128)S(1)}, f32[4,8,128]{2,1,0:T(8,128)}, u32[]{:S(2)}) copy-start(f32[4,8,128]{2,1,0:T(8,128)} %get-tuple-element.26) | copy-start | bytes 49156
  219.5 31.6 %copy-start.30 = (f32[4,8,128]{2,1,0:T(8,128)S(1)}, f32[4,8,128]{2,1,0:T(8,128)}, u32[]{:S(2)}) copy-start(f32[4,8,128]{2,1,0:T(8,128)} %get-tuple-element.27) | copy-start | bytes 49156
  219.5 31.6 %copy-start.31 = (f32[4,8,128]{2,1,0:T(8,128)S(1)}, f32[4,8,128]{2,1,0:T(8,128)}, u32[]{:S(2)}) copy-start(f32[4,8,128]{2,1,0:T(8,128)} %get-tuple-element.64) | copy-start | bytes 49156
  219.5 31.6 %copy-start.32 = (f32[4,8,128]{2,1,0:T(8,128)S(1)}, f32[4,8,128]{2,1,0:T(8,128)}, u32[]{:S(2)}) copy-start(f32[4,8,128]{2,1,0:T(8,128)} %get-tuple-element.65) | copy-start | bytes 49156
  220.6 5.3 %collective-permute-start.16 = (f32[8,1,8,128]{3,2,1,0:T(8,128)S(1)}, f32[8,1,8,128]{3,2,1,0:T(8,128)S(1)}, u32[]{:S(2)}, u32[]{:S(2)}) collective-permute-start(f32[8,1,8,128]{3,2,1,0:T(8,128)S(1)} %get-tuple-element.61), channel_id=1, source_target_pairs={{16,0},{32,16},{48,32},{64,48},{80,64},{96,80},{112,96},{128,112},... | collective-permute-start | bytes 98312 | tf_op jit(solution)/shard_map/ppermute | solution.py:27
  221.9 5.0 %collective-permute-start.17 = (f32[8,1,8,128]{3,2,1,0:T(8,128)S(1)}, f32[8,1,8,128]{3,2,1,0:T(8,128)S(1)}, u32[]{:S(2)}, u32[]{:S(2)}) collective-permute-start(f32[8,1,8,128]{3,2,1,0:T(8,128)S(1)} %get-tuple-element.60), channel_id=1, source_target_pairs={{0,16},{16,32},{32,48},{48,64},{64,80},{80,96},{96,112},{112,128},... | collective-permute-start | bytes 98312 | tf_op jit(solution)/shard_map/ppermute | solution.py:25
  226.9 7.3 %collective-permute-start.18 = (f32[8,6,1,128]{3,2,1,0:T(1,128)S(1)}, f32[8,6,1,128]{3,2,1,0:T(1,128)S(1)}, u32[]{:S(2)}, u32[]{:S(2)}) collective-permute-start(f32[8,6,1,128]{3,2,1,0:T(1,128)S(1)} %get-tuple-element.54), channel_id=1, source_target_pairs={{1,0},{2,1},{3,2},{4,3},{5,4},{6,5},{7,6},{8,7},{9,8},{10,9},{11,1... | collective-permute-start | bytes 73736 | tf_op jit(solution)/shard_map/ppermute | solution.py:27
  230.4 4.8 %collective-permute-start.19 = (f32[8,6,1,128]{3,2,1,0:T(1,128)S(1)}, f32[8,6,1,128]{3,2,1,0:T(1,128)S(1)}, u32[]{:S(2)}, u32[]{:S(2)}) collective-permute-start(f32[8,6,1,128]{3,2,1,0:T(1,128)S(1)} %get-tuple-element.55), channel_id=1, source_target_pairs={{0,1},{1,2},{2,3},{3,4},{4,5},{5,6},{6,7},{7,8},{8,9},{9,10},{10,1... | collective-permute-start | bytes 73736 | tf_op jit(solution)/shard_map/ppermute | solution.py:25
  236.3 5.9 %collective-permute-start.20 = (f32[8,1,8,128]{3,2,1,0:T(8,128)S(1)}, f32[8,1,8,128]{3,2,1,0:T(8,128)S(1)}, u32[]{:S(2)}, u32[]{:S(2)}) collective-permute-start(f32[8,1,8,128]{3,2,1,0:T(8,128)S(1)} %get-tuple-element.59), channel_id=1, source_target_pairs={{16,0},{32,16},{48,32},{64,48},{80,64},{96,80},{112,96},{128,112},... | collective-permute-start | bytes 98312 | tf_op jit(solution)/shard_map/ppermute | solution.py:27
  237.6 5.6 %collective-permute-start.21 = (f32[8,1,8,128]{3,2,1,0:T(8,128)S(1)}, f32[8,1,8,128]{3,2,1,0:T(8,128)S(1)}, u32[]{:S(2)}, u32[]{:S(2)}) collective-permute-start(f32[8,1,8,128]{3,2,1,0:T(8,128)S(1)} %get-tuple-element.58), channel_id=1, source_target_pairs={{0,16},{16,32},{32,48},{48,64},{64,80},{80,96},{96,112},{112,128},... | collective-permute-start | bytes 98312 | tf_op jit(solution)/shard_map/ppermute | solution.py:25
  243.2 7.1 %collective-permute-start.22 = (f32[8,6,1,128]{3,2,1,0:T(1,128)S(1)}, f32[8,6,1,128]{3,2,1,0:T(1,128)S(1)}, u32[]{:S(2)}, u32[]{:S(2)}) collective-permute-start(f32[8,6,1,128]{3,2,1,0:T(1,128)S(1)} %get-tuple-element.52), channel_id=1, source_target_pairs={{1,0},{2,1},{3,2},{4,3},{5,4},{6,5},{7,6},{8,7},{9,8},{10,9},{11,1... | collective-permute-start | bytes 73736 | tf_op jit(solution)/shard_map/ppermute | solution.py:27
  245.1 6.0 %collective-permute-start.23 = (f32[8,6,1,128]{3,2,1,0:T(1,128)S(1)}, f32[8,6,1,128]{3,2,1,0:T(1,128)S(1)}, u32[]{:S(2)}, u32[]{:S(2)}) collective-permute-start(f32[8,6,1,128]{3,2,1,0:T(1,128)S(1)} %get-tuple-element.53), channel_id=1, source_target_pairs={{0,1},{1,2},{2,3},{3,4},{4,5},{5,6},{6,7},{7,8},{8,9},{9,10},{10,1... | collective-permute-start | bytes 73736 | tf_op jit(solution)/shard_map/ppermute | solution.py:25
  251.4 6.0 %collective-permute-start.24 = (f32[8,1,8,128]{3,2,1,0:T(8,128)S(1)}, f32[8,1,8,128]{3,2,1,0:T(8,128)S(1)}, u32[]{:S(2)}, u32[]{:S(2)}) collective-permute-start(f32[8,1,8,128]{3,2,1,0:T(8,128)S(1)} %get-tuple-element.57), channel_id=1, source_target_pairs={{16,0},{32,16},{48,32},{64,48},{80,64},{96,80},{112,96},{128,112},... | collective-permute-start | bytes 98312 | tf_op jit(solution)/shard_map/ppermute | solution.py:27
  252.7 5.7 %collective-permute-start.25 = (f32[8,1,8,128]{3,2,1,0:T(8,128)S(1)}, f32[8,1,8,128]{3,2,1,0:T(8,128)S(1)}, u32[]{:S(2)}, u32[]{:S(2)}) collective-permute-start(f32[8,1,8,128]{3,2,1,0:T(8,128)S(1)} %get-tuple-element.56), channel_id=1, source_target_pairs={{0,16},{16,32},{32,48},{48,64},{64,80},{80,96},{96,112},{112,128},... | collective-permute-start | bytes 98312 | tf_op jit(solution)/shard_map/ppermute | solution.py:25
  258.5 7.0 %collective-permute-start.26 = (f32[8,6,1,128]{3,2,1,0:T(1,128)S(1)}, f32[8,6,1,128]{3,2,1,0:T(1,128)S(1)}, u32[]{:S(2)}, u32[]{:S(2)}) collective-permute-start(f32[8,6,1,128]{3,2,1,0:T(1,128)S(1)} %get-tuple-element.50), channel_id=1, source_target_pairs={{1,0},{2,1},{3,2},{4,3},{5,4},{6,5},{7,6},{8,7},{9,8},{10,9},{11,1... | collective-permute-start | bytes 73736 | tf_op jit(solution)/shard_map/ppermute | solution.py:27
  260.4 6.0 %collective-permute-start.27 = (f32[8,6,1,128]{3,2,1,0:T(1,128)S(1)}, f32[8,6,1,128]{3,2,1,0:T(1,128)S(1)}, u32[]{:S(2)}, u32[]{:S(2)}) collective-permute-start(f32[8,6,1,128]{3,2,1,0:T(1,128)S(1)} %get-tuple-element.51), channel_id=1, source_target_pairs={{0,1},{1,2},{2,3},{3,4},{4,5},{5,6},{6,7},{7,8},{8,9},{9,10},{10,1... | collective-permute-start | bytes 73736 | tf_op jit(solution)/shard_map/ppermute | solution.py:25
  289.2 17.7 %copy-start.7 = (f32[8,16,256]{2,1,0:T(8,128)S(1)}, f32[8,16,256]{2,1,0:T(8,128)}, u32[]{:S(2)}) copy-start(f32[8,16,256]{2,1,0:T(8,128)} %get-tuple-element.30) | copy-start | bytes 393220
  289.3 17.7 %copy-start.9 = (f32[8,16,256]{2,1,0:T(8,128)S(1)}, f32[8,16,256]{2,1,0:T(8,128)}, u32[]{:S(2)}) copy-start(f32[8,16,256]{2,1,0:T(8,128)} %copy-done.8) | copy-start | bytes 393220
  289.3 17.7 %copy-start.13 = (f32[8,16,256]{2,1,0:T(8,128)S(1)}, f32[8,16,256]{2,1,0:T(8,128)}, u32[]{:S(2)}) copy-start(f32[8,16,256]{2,1,0:T(8,128)} %copy-done.11) | copy-start | bytes 393220
  289.3 17.7 %copy-start.16 = (f32[8,16,256]{2,1,0:T(8,128)S(1)}, f32[8,16,256]{2,1,0:T(8,128)}, u32[]{:S(2)}) copy-start(f32[8,16,256]{2,1,0:T(8,128)} %copy-done.14) | copy-start | bytes 393220
  289.3 17.7 %copy-start.19 = (f32[8,16,256]{2,1,0:T(8,128)S(1)}, f32[8,16,256]{2,1,0:T(8,128)}, u32[]{:S(2)}) copy-start(f32[8,16,256]{2,1,0:T(8,128)} %copy-done.17) | copy-start | bytes 393220
  289.3 6.4 %collective-permute-start.28 = (f32[8,1,16,256]{3,2,1,0:T(8,128)S(1)}, f32[8,1,16,256]{3,2,1,0:T(8,128)S(1)}, u32[]{:S(2)}, u32[]{:S(2)}) collective-permute-start(f32[8,1,16,256]{3,2,1,0:T(8,128)S(1)} %get-tuple-element.43), channel_id=1, source_target_pairs={{16,0},{32,16},{48,32},{64,48},{80,64},{96,80},{112,96},{128,112},... | collective-permute-start | bytes 393224 | tf_op jit(solution)/shard_map/ppermute | solution.py:27
  290.8 6.5 %collective-permute-start.29 = (f32[8,1,16,256]{3,2,1,0:T(8,128)S(1)}, f32[8,1,16,256]{3,2,1,0:T(8,128)S(1)}, u32[]{:S(2)}, u32[]{:S(2)}) collective-permute-start(f32[8,1,16,256]{3,2,1,0:T(8,128)S(1)} %get-tuple-element.42), channel_id=1, source_target_pairs={{0,16},{16,32},{32,48},{48,64},{64,80},{80,96},{96,112},{112,128},... | collective-permute-start | bytes 393224 | tf_op jit(solution)/shard_map/ppermute | solution.py:25
  297.4 8.3 %collective-permute-start.30 = (f32[8,10,1,256]{3,0,2,1:T(8,128)S(1)}, f32[8,10,1,256]{3,0,2,1:T(8,128)S(1)}, u32[]{:S(2)}, u32[]{:S(2)}) collective-permute-start(f32[8,10,1,256]{3,0,2,1:T(8,128)S(1)} %copy.453), channel_id=1, source_target_pairs={{1,0},{2,1},{3,2},{4,3},{5,4},{6,5},{7,6},{8,7},{9,8},{10,9},{11,1... | collective-permute-start | bytes 245768 | tf_op jit(solution)/shard_map/ppermute | solution.py:27
  299.3 7.6 %collective-permute-start.31 = (f32[8,10,1,256]{3,0,2,1:T(8,128)S(1)}, f32[8,10,1,256]{3,0,2,1:T(8,128)S(1)}, u32[]{:S(2)}, u32[]{:S(2)}) collective-permute-start(f32[8,10,1,256]{3,0,2,1:T(8,128)S(1)} %copy.455), channel_id=1, source_target_pairs={{0,1},{1,2},{2,3},{3,4},{4,5},{5,6},{6,7},{7,8},{8,9},{9,10},{10,1... | collective-permute-start | bytes 245768 | tf_op jit(solution)/shard_map/ppermute | solution.py:25
  (21 other events, 131.9 us)
